TPU v7x, 1024 devices: a whole 4x4x32 slice. The times are simulated.
1024 devices in a mesh: dp: 64 (over z, core), expert: 16 (over y, x).
Axes of the slice: x: 4, y: 4, z: 32, core: 2. Of those that a mesh axis runs over, the one named last changes fastest.
Arguments:
- latents: bfloat16 [131072, 512], P(('dp', 'expert')), may hold values from -6 to 6
- routes: int32 [131072, 3], P(('dp', 'expert')), may hold values from 0 to 15, all different within a row; in each aligned block of 128 rows (0 to 127, 128 to 255, ...) at most 32 rows name the same one
- gate_level: int32 [131072, 3], P(('dp', 'expert')), may hold values from 1 to 256
- cotangent: bfloat16 [131072, 512], P(('dp', 'expert')), may hold values from -6 to 6
- w_gate: bfloat16 [16, 512, 1024], P('expert'), may hold values from -0.25 to 0.25
- w_up: bfloat16 [16, 512, 1024], P('expert'), may hold values from -0.25 to 0.25
- w_down: bfloat16 [16, 1024, 512], P('expert'), may hold values from -0.1875 to 0.1875
Outputs:
- latent_out: bfloat16 [131072, 512], P(('dp', 'expert'))
- grad_latents: bfloat16 [131072, 512], P(('dp', 'expert'))
- grad_down: float32 [16, 1024, 512], P('expert', 'dp')
Inputs may be any that keep to these rules, and one draw needn't show every extreme that they name: `routes`: each row names 3 different experts; in the rows of one device no expert is named by more than 32 rows, and in every draw some expert is named by exactly 32 rows of some device.
All inputs are finite; a program needn't handle non-finite values.
Results may differ from a plain program's by a relative error of at most 0.0064.
Values may be sent and summed in bfloat16 or wider, within the bound.
A program may use at most 32 MiB of HBM per device.

v0:
```python
import jax
import jax.numpy as jnp
from jax import lax
from jax.sharding import PartitionSpec as P

CAP = 32


def local(latents, routes, gate_level, cotangent, w_gate, w_up, w_down):
    groups = lax.axis_size("expert")
    local_count = w_gate.shape[0]
    experts = groups * local_count
    tok_rows, feature_width = latents.shape
    route_count = routes.shape[1]
    slot_count = CAP
    flat_routes = routes.reshape(-1)
    expert_ids = jnp.arange(experts, dtype=jnp.int32)
    one_hot = (flat_routes[:, None] == expert_ids[None, :]).astype(jnp.int32)
    before = jnp.cumsum(one_hot, axis=0) - one_hot
    slot_index = jnp.sum(before * one_hot, axis=1)
    position = flat_routes * slot_count + slot_index
    targets = jnp.arange(experts * slot_count, dtype=jnp.int32)
    route_place = (position[None, :] == targets[:, None]).astype(jnp.bfloat16)
    levels = gate_level.astype(jnp.float32)
    weight = levels / jnp.sum(levels, axis=1, keepdims=True)
    scaled = (weight[:, :, None] * cotangent.astype(jnp.float32)[:, None, :]).astype(jnp.bfloat16)
    scaled = scaled.reshape(tok_rows * route_count, feature_width)
    token_rows = jnp.repeat(latents, route_count, axis=0)
    send_rows = jnp.dot(route_place, token_rows, preferred_element_type=jnp.float32).astype(
        jnp.bfloat16
    )
    send_grad = jnp.dot(route_place, scaled, preferred_element_type=jnp.float32).astype(
        jnp.bfloat16
    )
    send_rows = send_rows.reshape(experts, slot_count, feature_width)
    send_grad = send_grad.reshape(experts, slot_count, feature_width)

    def to_experts(arrived):
        shaped = arrived.reshape(groups, local_count, slot_count, arrived.shape[-1])
        return shaped.transpose(1, 0, 2, 3).reshape(
            local_count, groups * slot_count, arrived.shape[-1]
        )

    def to_sources(result):
        shaped = result.reshape(local_count, groups, slot_count, result.shape[-1])
        return shaped.transpose(1, 0, 2, 3).reshape(
            groups * local_count, slot_count, result.shape[-1]
        )

    def collect(arrived):
        picked = jnp.dot(
            route_place.T, arrived.reshape(-1, feature_width), preferred_element_type=jnp.float32
        )
        return picked.reshape(tok_rows, route_count, feature_width)

    arrived_rows = lax.all_to_all(send_rows, "expert", split_axis=0, concat_axis=0, tiled=True)
    expert_rows = to_experts(arrived_rows)
    gate_pre = jnp.einsum("erl,elh->erh", expert_rows, w_gate, preferred_element_type=jnp.float32)
    up_pre = jnp.einsum("erl,elh->erh", expert_rows, w_up, preferred_element_type=jnp.float32)
    sigmoid_gate = jax.nn.sigmoid(gate_pre)
    activated = gate_pre * sigmoid_gate
    hidden = (activated * up_pre).astype(jnp.bfloat16)
    expert_out = jnp.einsum(
        "erh,ehl->erl", hidden, w_down, preferred_element_type=jnp.float32
    ).astype(jnp.bfloat16)
    returned = lax.all_to_all(
        to_sources(expert_out), "expert", split_axis=0, concat_axis=0, tiled=True
    )
    latent_out = jnp.sum(weight[:, :, None] * collect(returned), axis=1).astype(jnp.bfloat16)
    arrived_grad = lax.all_to_all(send_grad, "expert", split_axis=0, concat_axis=0, tiled=True)
    row_grad = to_experts(arrived_grad)
    grad_term = jnp.einsum("erh,erl->ehl", hidden, row_grad, preferred_element_type=jnp.float32)
    grad_down = lax.psum_scatter(grad_term, "dp", scatter_dimension=1, tiled=True)
    hidden_grad = jnp.einsum("erl,ehl->erh", row_grad, w_down, preferred_element_type=jnp.float32)
    derivative = sigmoid_gate * (1.0 + gate_pre * (1.0 - sigmoid_gate))
    gate_grad = (hidden_grad * up_pre * derivative).astype(jnp.bfloat16)
    up_grad = (hidden_grad * activated).astype(jnp.bfloat16)
    row_input = (
        jnp.einsum("erh,elh->erl", gate_grad, w_gate, preferred_element_type=jnp.float32)
        + jnp.einsum("erh,elh->erl", up_grad, w_up, preferred_element_type=jnp.float32)
    ).astype(jnp.bfloat16)
    grad_back = lax.all_to_all(
        to_sources(row_input), "expert", split_axis=0, concat_axis=0, tiled=True
    )
    grad_latents = jnp.sum(collect(grad_back), axis=1).astype(jnp.bfloat16)
    return (latent_out, grad_latents, grad_down)


def solution(mesh):
    return jax.shard_map(
        local,
        mesh=mesh,
        in_specs=(
            P(("dp", "expert"), None),
            P(("dp", "expert"), None),
            P(("dp", "expert"), None),
            P(("dp", "expert"), None),
            P("expert", None, None),
            P("expert", None, None),
            P("expert", None, None),
        ),
        out_specs=(P(("dp", "expert"), None), P(("dp", "expert"), None), P("expert", "dp", None)),
        check_vma=False,
    )
```

profile of v0, /device:TPU:4, one launch (start us, length us, event | category | flops | bytes accessed | tf_op | source)
XLA Modules:
  0.0 270.5 jit_solution(11205288984175177926)
XLA Ops:
  7.2 0.9 copy.17
  8.5 0.9 reduce-window.6
  9.7 1.0 broadcast_in_dim.2
  11.1 1.3 convolution_convert_fusion.1
  12.4 16.5 %all-to-all-start = ((bf16[16,32,512]{2,1,0:T(8,128)(2,1)}), bf16[16,32,512]{2,1,0:T(8,128)(2,1)S(1)}, u32[]{:S(2)}, u32[]{:S(2)}) async-start(bf16[16,32,512]{2,1,0:T(8,128)(2,1)} %bitcast.2), calls=%async_computation | async-start | bytes 1048576 | tf_op jit(solution)/shard_map/all_to_all | solution.py:56
  29.8 1.3 convolution_convert_fusion
  31.1 5.7 %all-to-all-done = bf16[16,32,512]{2,1,0:T(8,128)(2,1)S(1)} async-done(((bf16[16,32,512]{2,1,0:T(8,128)(2,1)}), bf16[16,32,512]{2,1,0:T(8,128)(2,1)S(1)}, u32[]{:S(2)}, u32[]{:S(2)}) %all-to-all-start) | async-done | bytes 524320 | tf_op jit(solution)/shard_map/all_to_all | solution.py:56
  36.8 6.9 %all-to-all-start.2 = ((bf16[16,32,512]{2,1,0:T(8,128)(2,1)}), bf16[16,32,512]{2,1,0:T(8,128)(2,1)S(1)}, u32[]{:S(2)}, u32[]{:S(2)}) async-start(bf16[16,32,512]{2,1,0:T(8,128)(2,1)} %bitcast.10), calls=%async_computation.2 | async-start | bytes 1048576 | tf_op jit(solution)/shard_map/all_to_all | solution.py:70
  43.7 1.9 fusion.11
  45.7 1.3 copy-done.1
  47.0 2.5 multiply_convert_fusion.2
  49.5 1.7 all-to-all-done.2
  51.3 3.4 %convolution_bitcast_fusion = f32[1,1024,512]{2,1,0:T(8,128)} fusion(bf16[512,1024]{1,0:T(8,128)(2,1)} %get-tuple-element.3, bf16[512,512]{1,0:T(8,128)(2,1)S(1)} %bitcast.64), kind=kOutput, calls=%fused_computation.5 | convolution fusion | flops 536870912 | bytes 3670016 | tf_op jit(solution)/shard_map/erh,erl->ehl/dot_general | solution.py:72
  55.5 0.8 copy-done.2
  56.6 2.6 fusion.9
  59.2 1.6 fusion.1
  60.8 6.7 %all-to-all-start.3 = ((bf16[16,32,512]{2,1,0:T(8,128)(2,1)}), bf16[16,32,512]{2,1,0:T(8,128)(2,1)}, u32[]{:S(2)}, u32[]{:S(2)}) async-start(bf16[16,32,512]{2,1,0:T(8,128)(2,1)} %bitcast.70), calls=%async_computation.3 | async-start | bytes 1048576 | tf_op jit(solution)/shard_map/all_to_all | solution.py:82
  67.5 1.5 convolution_convert_fusion.2
  69.0 8.5 %all-to-all-done.3 = bf16[16,32,512]{2,1,0:T(8,128)(2,1)} async-done(((bf16[16,32,512]{2,1,0:T(8,128)(2,1)}), bf16[16,32,512]{2,1,0:T(8,128)(2,1)}, u32[]{:S(2)}, u32[]{:S(2)}) %all-to-all-start.3) | async-done | bytes 524320 | tf_op jit(solution)/shard_map/all_to_all | solution.py:82
  77.5 6.1 %all-to-all-start.1 = ((bf16[16,32,512]{2,1,0:T(8,128)(2,1)}), bf16[16,32,512]{2,1,0:T(8,128)(2,1)S(1)}, u32[]{:S(2)}, u32[]{:S(2)}) async-start(bf16[16,32,512]{2,1,0:T(8,128)(2,1)} %bitcast.68), calls=%async_computation.1 | async-start | bytes 1048576 | tf_op jit(solution)/shard_map/all_to_all | solution.py:66
  83.9 2.2 convolution_reduce_fusion
  86.0 5.1 %all-to-all-done.1 = bf16[16,32,512]{2,1,0:T(8,128)(2,1)S(1)} async-done(((bf16[16,32,512]{2,1,0:T(8,128)(2,1)}), bf16[16,32,512]{2,1,0:T(8,128)(2,1)S(1)}, u32[]{:S(2)}, u32[]{:S(2)}) %all-to-all-start.1) | async-done | bytes 524320 | tf_op jit(solution)/shard_map/all_to_all | solution.py:66
  91.2 1.1 fusion.2
  92.2 171.5 %reduce-scatter.2.cloned.1.call-done = f32[1,16,512]{2,1,0:T(8,128)} async-done(((f32[1,1024,512]{2,1,0:T(8,128)}), f32[1,16,512]{2,1,0:T(8,128)}) %reduce-scatter.2.cloned.1.call-update) | async-done | bytes 32784 | tf_op jit(solution)/shard_map/reduce_scatter | solution.py:73
  (36 shorter events, 3.3 us)
Async XLA Ops:
  7.2 39.9 %copy-start = (bf16[1,512,1024]{2,1,0:T(8,128)(2,1)S(1)}, bf16[1,512,1024]{2,1,0:T(8,128)(2,1)}, u32[]{:S(2)}) copy-start(bf16[1,512,1024]{2,1,0:T(8,128)(2,1)} %param.12) | copy-start | bytes 3145732
  7.2 21.7 %copy-start.8 = (s32[128,3]{0,1:T(4,128)S(1)}, s32[128,3]{0,1:T(4,128)}, u32[]{:S(2)}) copy-start(s32[128,3]{0,1:T(4,128)} %param.9) | copy-start | bytes 4612
  7.2 22.1 %copy-start.6 = (bf16[128,512]{1,0:T(8,128)(2,1)S(1)}, bf16[128,512]{1,0:T(8,128)(2,1)}, u32[]{:S(2)}) copy-start(bf16[128,512]{1,0:T(8,128)(2,1)} %param.10) | copy-start | bytes 393220
  12.4 24.4 %all-to-all-start = ((bf16[16,32,512]{2,1,0:T(8,128)(2,1)}), bf16[16,32,512]{2,1,0:T(8,128)(2,1)S(1)}, u32[]{:S(2)}, u32[]{:S(2)}) async-start(bf16[16,32,512]{2,1,0:T(8,128)(2,1)} %bitcast.2), calls=%async_computation | async-start | bytes 1048576 | tf_op jit(solution)/shard_map/all_to_all | solution.py:56
  36.8 14.4 %all-to-all-start.2 = ((bf16[16,32,512]{2,1,0:T(8,128)(2,1)}), bf16[16,32,512]{2,1,0:T(8,128)(2,1)S(1)}, u32[]{:S(2)}, u32[]{:S(2)}) async-start(bf16[16,32,512]{2,1,0:T(8,128)(2,1)} %bitcast.10), calls=%async_computation.2 | async-start | bytes 1048576 | tf_op jit(solution)/shard_map/all_to_all | solution.py:70
  43.7 220.0 %reduce-scatter.2.cloned.1.call-start = ((), (), s32[]{:S(2)}) async-start(), calls=%async_computation.5 | async-start | bytes 2129920 | tf_op jit(solution)/shard_map/reduce_scatter | solution.py:73
  45.7 1.3 copy-start.1
  51.3 3.4 %copy-start.4 = (bf16[1,1024,512]{2,1,0:T(8,128)(2,1)S(1)}, bf16[1,1024,512]{2,1,0:T(8,128)(2,1)}, u32[]{:S(2)}) copy-start(bf16[1,1024,512]{2,1,0:T(8,128)(2,1)} %param.13) | copy-start | bytes 3145732
  54.7 1.6 copy-start.2
  54.7 1.8 copy-start.3
  59.2 8.3 %copy-start.5 = (bf16[512,1024]{1,0:T(8,128)(2,1)S(1)}, bf16[512,1024]{1,0:T(8,128)(2,1)}, u32[]{:S(2)}) copy-start(bf16[512,1024]{1,0:T(8,128)(2,1)} %get-tuple-element.3) | copy-start | bytes 3145732
  60.8 16.7 %all-to-all-start.3 = ((bf16[16,32,512]{2,1,0:T(8,128)(2,1)}), bf16[16,32,512]{2,1,0:T(8,128)(2,1)}, u32[]{:S(2)}, u32[]{:S(2)}) async-start(bf16[16,32,512]{2,1,0:T(8,128)(2,1)} %bitcast.70), calls=%async_computation.3 | async-start | bytes 1048576 | tf_op jit(solution)/shard_map/all_to_all | solution.py:82
  67.5 16.4 %copy-start.7 = (s32[128,3]{0,1:T(4,128)S(1)}, s32[128,3]{0,1:T(4,128)}, u32[]{:S(2)}) copy-start(s32[128,3]{0,1:T(4,128)} %param.8) | copy-start | bytes 4612
  77.5 13.7 %all-to-all-start.1 = ((bf16[16,32,512]{2,1,0:T(8,128)(2,1)}), bf16[16,32,512]{2,1,0:T(8,128)(2,1)S(1)}, u32[]{:S(2)}, u32[]{:S(2)}) async-start(bf16[16,32,512]{2,1,0:T(8,128)(2,1)} %bitcast.68), calls=%async_computation.1 | async-start | bytes 1048576 | tf_op jit(solution)/shard_map/all_to_all | solution.py:66
Sparse Core Ops, SparseCore 0:
  54.8 208.8 reduce-scatter.1
where the time goes:
time: 271 us
  waiting for transfers between devices  192 us (71%)
  starting transfers between devices  36.3 us (13%)
  matrix products  20.1 us (7%)
  between operations  14.2 us (5%)
  local copies, waits for them, and re-layouts  6.44 us (2%)
    reduce_scatter x1, waiting for transfers between devices, local(): lax.psum_scatter(grad_term, 'dp', scatter_dimension=1, tiled=True)  171 us
    all_to_all x1, starting transfers between devices, local(): lax.all_to_all(send_rows, 'expert', split_axis=0, concat_axis=0, tiled=True)  16.5 us
    all_to_all x1, waiting for transfers between devices, local(): lax.all_to_all(to_sources(row_input), 'expert', split_axis=0, concat_axis...  8.47 us
    all_to_all x1, starting transfers between devices, local(): lax.all_to_all(send_grad, 'expert', split_axis=0, concat_axis=0, tiled=True)  6.88 us
    all_to_all x1, starting transfers between devices, local(): lax.all_to_all(to_sources(row_input), 'expert', split_axis=0, concat_axis...  6.72 us
    all_to_all x1, starting transfers between devices, local(): lax.all_to_all(to_sources(expert_out), 'expert', split_axis=0, concat_axi...  6.12 us
    all_to_all x1, waiting for transfers between devices, local(): lax.all_to_all(send_rows, 'expert', split_axis=0, concat_axis=0, tiled=True)  5.69 us
  transfers between devices with their start and end apart: 5, of which 5 were waited for; matrix products, arithmetic and copies ran while one was open for 6% of the time, Pallas kernels for 0%

commit v1 on v0

v1 whole, which is shorter than its diff:
```python
import jax
import jax.numpy as jnp
from jax import lax
from jax.experimental import pallas as pl
from jax.experimental.pallas import tpu as pltpu
from jax.sharding import PartitionSpec as P

CAP = 32
SIDE = 4
F32 = jnp.float32
BF16 = jnp.bfloat16
MESH = pl.DeviceIdType.MESH


def ring_distance(step):
    return min(step, SIDE - step)


PLACES = sorted(
    [(dy, dx) for dy in range(SIDE) for dx in range(SIDE)],
    key=lambda o: (ring_distance(o[0]) + ring_distance(o[1]), o),
)
SLOTS = len(PLACES)
FAR_FIRST = list(range(SLOTS - 1, 0, -1))
GROUP = 8
GROUPS = SLOTS // GROUP
ROWS = GROUP * CAP

PARENT = {}
for _r in range(-16, 16):
    if _r % 3:
        PARENT[_r] = _r - 1 if _r % 3 == 1 else _r + 1
for _r in (-15, -12, -6, 6, 12, 15):
    PARENT[_r] = 9 if _r > 0 else -9
PARENT.update({3: 0, -3: 0, 9: 0, -9: 0})
CHILDREN = {}
for _r, _q in PARENT.items():
    CHILDREN.setdefault(_q, []).append(_r)
ORDER = [15, -15, 12, -12, 6, -6, 9, -9, 3, -3, 0]
FIRST = [r for q in ORDER for r in CHILDREN[q] if r % 3]
SECOND = [15, -15, 12, -12, 6, -6, 3, -3]
THIRD = [9, -9]
HOPS = FIRST + SECOND + THIRD
HOP_AT = {r: i for i, r in enumerate(HOPS)}
Z_NEAR = (1, -1, 3, -3, 6, -6)


def kernel(
    lat_hbm, routes_hbm, level_hbm, cot_hbm, wg_hbm, wu_hbm, wd_hbm,
    out_ref, grad_ref, down_ref,
    lat, routes, level, cot, wg, wu, wd,
    key, share, place, place_w,
    sx, rx, sg, rg, se, re, si, ri,
    hid, hid_t, act, rate,
    own, sc, rc, hop_s, hop_r,
    load_sem, x_sem, g_sem, e_sem, i_sem, c_sem, h_sem,
):
    dp, ex = lax.axis_index("dp"), lax.axis_index("expert")
    z_count = lax.axis_size("dp") // 2
    z, c = dp // 2, lax.rem(dp, 2)
    y, x = ex // SIDE, lax.rem(ex, SIDE)

    def at_place(place_index, sign):
        dy, dx = PLACES[place_index]
        return lax.rem(y + sign * dy + SIDE, SIDE) * SIDE + lax.rem(x + sign * dx + SIDE, SIDE)

    def at_z(shift):
        return (lax.rem(z + shift + z_count, z_count) * 2 + c, ex)

    barrier = pltpu.get_barrier_semaphore()
    greeted = [(dp, at_place(j, 1)) for j in range(1, SLOTS)]
    greeted += [at_z(d) for d in Z_NEAR] + [(z * 2 + 1 - c, ex)]
    for device in greeted:
        pl.semaphore_signal(barrier, inc=1, device_id=device, device_id_type=MESH)

    loads = [
        pltpu.make_async_copy(source, target, load_sem.at[i])
        for i, (source, target) in enumerate(
            ((routes_hbm, routes), (level_hbm, level), (lat_hbm, lat), (cot_hbm, cot),
             (wg_hbm, wg), (wu_hbm, wu), (wd_hbm, wd))
        )
    ]
    for load in loads:
        load.start()
    loads[0].wait()
    loads[1].wait()

    tokens = lat.shape[0]
    lane = lax.broadcasted_iota(jnp.int32, (tokens, tokens), 1)
    row = lax.broadcasted_iota(jnp.int32, (tokens, tokens), 0)
    expert = lax.broadcasted_iota(jnp.int32, (SLOTS, tokens), 0)
    named = routes[...]
    levels = level[...].astype(F32)
    weight = levels / (levels[0:1] + levels[1:2] + levels[2:3])
    chosen_t = jnp.zeros((SLOTS, tokens), F32)
    share_t = jnp.zeros((SLOTS, tokens), F32)
    for k in range(3):
        hit = named[k:k + 1] == expert
        chosen_t = jnp.where(hit, 1.0, chosen_t)
        share_t = jnp.where(hit, weight[k:k + 1], share_t)
    share[...] = share_t
    earlier = (row < lane).astype(F32).astype(BF16)
    before = jnp.dot(chosen_t.astype(BF16), earlier, preferred_element_type=F32)
    key[...] = jnp.where(chosen_t > 0.0, before, -1.0)
    slot_of = lax.broadcasted_iota(jnp.int32, (CAP, tokens), 0).astype(F32)
    for j in range(SLOTS):
        e = at_place(j, 1)
        taken = key[pl.ds(e, 1), :] == slot_of
        place[j] = jnp.where(taken, 1.0, 0.0).astype(BF16)
        place_w[j] = jnp.where(taken, share[pl.ds(e, 1), :], 0.0)

    whole = SLOTS * CAP
    width = lat.shape[1]
    loads[2].wait()
    picked = place[...].reshape(whole, tokens)
    sx[...] = jnp.dot(picked, lat[...], preferred_element_type=F32).astype(BF16).reshape(
        SLOTS, CAP, width)

    def send(source, target, sems, j, sign):
        copy = pltpu.make_async_remote_copy(
            source.at[j], target.at[j], sems.at[0, j], sems.at[1, j],
            device_id=(dp, at_place(j, sign)), device_id_type=MESH)
        copy.start()
        return copy

    pl.semaphore_wait(barrier, len(greeted))
    x_copies = {j: send(sx, rx, x_sem, j, 1) for j in FAR_FIRST}
    rx[0] = sx[0]
    loads[3].wait()
    row_weight = jnp.sum(place_w[...].reshape(whole, tokens), axis=1, keepdims=True)
    scaled = row_weight * jnp.dot(picked, cot[...], preferred_element_type=F32)
    sg[...] = scaled.astype(BF16).reshape(SLOTS, CAP, width)
    g_copies = {j: send(sg, rg, g_sem, j, 1) for j in FAR_FIRST}
    rg[0] = sg[0]

    spread_w = place_w[...].reshape(whole, tokens).T
    high = spread_w.astype(BF16)
    low = (spread_w - high.astype(F32)).astype(BF16)
    spread_one = place[...].astype(F32).reshape(whole, tokens).T.astype(BF16)

    for load in loads[4:]:
        load.wait()
    hidden_width = wg.shape[1]
    tile = 256
    e_copies, i_copies = {}, {}
    for g in range(GROUPS):
        members = range(g * GROUP, (g + 1) * GROUP)
        for j in members:
            if j:
                x_copies[j].wait_recv()
        rows_in = rx[g * GROUP:(g + 1) * GROUP].reshape(ROWS, width)
        span = slice(g * ROWS, (g + 1) * ROWS)
        for n in range(hidden_width // tile):
            cols = slice(n * tile, (n + 1) * tile)
            gate = jnp.dot(rows_in, wg[:, cols], preferred_element_type=F32)
            up = jnp.dot(rows_in, wu[:, cols], preferred_element_type=F32)
            sig = jax.nn.sigmoid(gate)
            activated = gate * sig
            hidden = activated * up
            act[span, cols] = activated
            rate[span, cols] = up * (sig * (1.0 + gate * (1.0 - sig)))
            hid[:, cols] = hidden.astype(BF16)
            turned = hidden.T.astype(BF16).reshape(tile // 32, 2, 16, ROWS)
            chunk = slice(n * (tile // 32), (n + 1) * (tile // 32))
            hid_t[0, chunk, :, span] = turned[:, 0]
            hid_t[1, chunk, :, span] = turned[:, 1]
        result = jnp.dot(hid[...], wd[...], preferred_element_type=F32)
        se[g * GROUP:(g + 1) * GROUP] = result.astype(BF16).reshape(GROUP, CAP, width)
        for j in reversed(members):
            if j:
                e_copies[j] = send(se, re, e_sem, j, -1)
    re[0] = se[0]

    for j in range(1, SLOTS):
        g_copies[j].wait_recv()
    grads = rg[...].reshape(whole, width)
    half = z_count // 2
    c_copies = []
    for i in range(2):
        part = slice(i * half, (i + 1) * half)
        lhs = hid_t[1 - c, part].reshape(half * 16, whole)
        term = jnp.dot(lhs, grads, preferred_element_type=F32)
        sc[part] = term.astype(BF16).reshape(half, 16, width)
        copy = pltpu.make_async_remote_copy(
            sc.at[part], rc.at[part], c_sem.at[0, i], c_sem.at[1, i],
            device_id=(z * 2 + 1 - c, ex), device_id_type=MESH)
        copy.start()
        c_copies.append(copy)
    for i in range(2):
        part = slice(i * half, (i + 1) * half)
        lhs = hid_t[c, part].reshape(half * 16, whole)
        own[part] = jnp.dot(lhs, grads, preferred_element_type=F32).reshape(half, 16, width)

    def backward(g):
        members = range(g * GROUP, (g + 1) * GROUP)
        span = slice(g * ROWS, (g + 1) * ROWS)
        row_grad = rg[g * GROUP:(g + 1) * GROUP].reshape(ROWS, width)
        total = jnp.zeros((ROWS, width), F32)
        turn = (((1,), (1,)), ((), ()))
        for n in range(hidden_width // tile):
            cols = slice(n * tile, (n + 1) * tile)
            back = lax.dot_general(row_grad, wd[cols, :], turn, preferred_element_type=F32)
            gate_grad = (back * rate[span, cols]).astype(BF16)
            up_grad = (back * act[span, cols]).astype(BF16)
            total += lax.dot_general(gate_grad, wg[:, cols], turn, preferred_element_type=F32)
            total += lax.dot_general(up_grad, wu[:, cols], turn, preferred_element_type=F32)
        si[g * GROUP:(g + 1) * GROUP] = total.astype(BF16).reshape(GROUP, CAP, width)
        for j in reversed(members):
            if j:
                i_copies[j] = send(si, ri, i_sem, j, -1)

    hops = {}

    def partial(r):
        d = lax.rem(z - r + z_count, z_count)
        value = own[d] + rc[d].astype(F32)
        for child in CHILDREN.get(r, ()):
            hops[child].wait_recv()
            value = value + hop_r[HOP_AT[child]].astype(F32)
        return value

    def hop(r):
        i = HOP_AT[r]
        hop_s[i] = partial(r).astype(BF16)
        copy = pltpu.make_async_remote_copy(
            hop_s.at[i], hop_r.at[i], h_sem.at[0, i], h_sem.at[1, i],
            device_id=at_z(PARENT[r] - r), device_id_type=MESH)
        copy.start()
        hops[r] = copy

    backward(0)
    for copy in c_copies:
        copy.wait_recv()
    for r in FIRST:
        hop(r)
    backward(1)
    ri[0] = si[0]
    for r in SECOND:
        hop(r)
    for j in range(1, SLOTS):
        e_copies[j].wait_recv()
    returned = re[...].reshape(whole, width)
    summed = jnp.dot(high, returned, preferred_element_type=F32)
    summed += jnp.dot(low, returned, preferred_element_type=F32)
    out_ref[...] = summed.astype(BF16)
    for r in THIRD:
        hop(r)
    for j in range(1, SLOTS):
        i_copies[j].wait_recv()
    grad_ref[...] = jnp.dot(
        spread_one, ri[...].reshape(whole, width), preferred_element_type=F32).astype(BF16)
    down_ref[...] = partial(0)

    for copies in (x_copies, g_copies, e_copies, i_copies, hops):
        for copy in copies.values():
            copy.wait_send()
    for copy in c_copies:
        copy.wait_send()


def local(latents, routes, gate_level, cotangent, w_gate, w_up, w_down):
    tokens, width = latents.shape
    hidden = w_gate.shape[2]
    whole = SLOTS * CAP
    z_count = lax.axis_size("dp") // 2
    block = (SLOTS, CAP, width)
    hop_count = len(HOPS)
    anywhere = pl.BlockSpec(memory_space=pl.ANY)
    in_vmem = pl.BlockSpec(memory_space=pltpu.VMEM)
    dma = pltpu.SemaphoreType.DMA
    latent_out, grad_latents, grad_down = pl.pallas_call(
        kernel,
        out_shape=(
            jax.ShapeDtypeStruct((tokens, width), BF16),
            jax.ShapeDtypeStruct((tokens, width), BF16),
            jax.ShapeDtypeStruct((16, width), F32),
        ),
        in_specs=[anywhere] * 7,
        out_specs=(in_vmem,) * 3,
        scratch_shapes=[
            pltpu.VMEM(latents.shape, BF16),
            pltpu.VMEM(routes.shape[::-1], jnp.int32),
            pltpu.VMEM(gate_level.shape[::-1], jnp.int32),
            pltpu.VMEM(cotangent.shape, BF16),
            pltpu.VMEM((width, hidden), BF16),
            pltpu.VMEM((width, hidden), BF16),
            pltpu.VMEM((hidden, width), BF16),
            pltpu.VMEM((SLOTS, tokens), F32),
            pltpu.VMEM((SLOTS, tokens), F32),
            pltpu.VMEM((SLOTS, CAP, tokens), BF16),
            pltpu.VMEM((SLOTS, CAP, tokens), F32),
        ] + [pltpu.VMEM(block, BF16)] * 8 + [
            pltpu.VMEM((ROWS, hidden), BF16),
            pltpu.VMEM((2, z_count, 16, whole), BF16),
            pltpu.VMEM((whole, hidden), F32),
            pltpu.VMEM((whole, hidden), F32),
            pltpu.VMEM((z_count, 16, width), F32),
            pltpu.VMEM((z_count, 16, width), BF16),
            pltpu.VMEM((z_count, 16, width), BF16),
            pltpu.VMEM((hop_count, 16, width), BF16),
            pltpu.VMEM((hop_count, 16, width), BF16),
            dma((7,)), dma((2, SLOTS)), dma((2, SLOTS)), dma((2, SLOTS)), dma((2, SLOTS)),
            dma((2, 2)), dma((2, hop_count)),
        ],
        compiler_params=pltpu.CompilerParams(
            collective_id=0, has_side_effects=True, vmem_limit_bytes=56 << 20),
        name="moe",
    )(latents, routes.T, gate_level.T, cotangent, w_gate[0], w_up[0], w_down[0])
    return latent_out, grad_latents, grad_down[None]


def solution(mesh):
    return jax.shard_map(
        local,
        mesh=mesh,
        in_specs=(
            P(("dp", "expert"), None),
            P(("dp", "expert"), None),
            P(("dp", "expert"), None),
            P(("dp", "expert"), None),
            P("expert", None, None),
            P("expert", None, None),
            P("expert", None, None),
        ),
        out_specs=(P(("dp", "expert"), None), P(("dp", "expert"), None), P("expert", "dp", None)),
        check_vma=False,
    )
```

time: 271 us -> 67.9 us (0.25)
  the two profiles are of different devices: /device:TPU:4 before, /device:TPU:14 now
where the time goes in v1:
time: 67.9 us; the launch traced here: 67.7 us
  Pallas kernels  64.1 us (94%)
  local copies, waits for them, and re-layouts  2.98 us (4%)
    pallas_call x1, Pallas kernels, local(): pl.pallas_call(kernel, out_shape=(jax.ShapeDtypeStruct((tokens, width), B...  64.1 us
    unnamed x7, local copies, waits for them, and re-layouts  2.98 us

profile of v1, /device:TPU:14, one launch (start us, length us, event | category | flops | bytes accessed | tf_op | source)
XLA Modules:
  0.0 67.7 jit_solution(5756895105719415007)
XLA Ops:
  0.6 64.1 %moe.1 = (bf16[128,512]{1,0:T(8,128)(2,1)}, bf16[128,512]{1,0:T(8,128)(2,1)}, f32[16,512]{1,0:T(8,128)}) custom-call(bf16[128,512]{1,0:T(8,128)(2,1)} %lat_hbm.1, s32[3,128]{1,0:T(4,128)} %bitcast.10, s32[3,128]{1,0:T(4,128)} %bitcast.11, bf16[128,512]{1,0:T(8,128)(2,1)} %cot_hbm.1, bf16[512,1024]{1,0:T(8,128)(2,1)} %bitcast.6, bf16[512,1024]{1,0:T(8,128)(2,1)} %bitcast.7, ...), custom_call_target="tpu_custom_call" | custom-call | tf_op jit(solution)/shard_map/moe/pallas_call | solution.py:271
  64.7 0.0 copy-start
  64.7 1.6 %copy.13 = bf16[128,512]{1,0:T(8,128)(2,1)} copy(bf16[128,512]{1,0:T(8,128)(2,1)} %get-tuple-element.12) | data formatting | bytes 262144
  66.3 0.0 copy-done
  66.3 0.0 copy-start.1
  66.3 0.7 copy.14
  67.0 0.1 copy-done.1
  67.1 0.6 copy.15
Async XLA Ops:
  64.7 1.6 %copy-start = (bf16[128,512]{1,0:T(8,128)(2,1)S(1)}, bf16[128,512]{1,0:T(8,128)(2,1)}, u32[]{:S(2)}) copy-start(bf16[128,512]{1,0:T(8,128)(2,1)} %get-tuple-element.13) | copy-start | bytes 393220
  66.3 0.8 %copy-start.1 = (f32[16,512]{1,0:T(8,128)S(1)}, f32[16,512]{1,0:T(8,128)}, u32[]{:S(2)}) copy-start(f32[16,512]{1,0:T(8,128)} %get-tuple-element.8) | copy-start | bytes 98308

commit v2 on v1

--- a/solution.py
+++ b/solution.py
@@ -21,28 +21,25 @@
     key=lambda o: (ring_distance(o[0]) + ring_distance(o[1]), o),
 )
 SLOTS = len(PLACES)
-FAR_FIRST = list(range(SLOTS - 1, 0, -1))
 GROUP = 8
 GROUPS = SLOTS // GROUP
 ROWS = GROUP * CAP
 
 PARENT = {}
-for _r in range(-16, 16):
-    if _r % 3:
-        PARENT[_r] = _r - 1 if _r % 3 == 1 else _r + 1
-for _r in (-15, -12, -6, 6, 12, 15):
-    PARENT[_r] = 9 if _r > 0 else -9
-PARENT.update({3: 0, -3: 0, 9: 0, -9: 0})
+for _r, _q in {
+    1: 0, 2: 1, 3: 2, 4: 0, 5: 4, 6: 5, 7: 9, 8: 9, 9: 10, 10: 0, 11: 10, 12: 10, 13: 14, 14: 10, 15: 14,
+}.items():
+    PARENT[_r], PARENT[-_r] = _q, -_q
+PARENT[-16] = -14
 CHILDREN = {}
 for _r, _q in PARENT.items():
     CHILDREN.setdefault(_q, []).append(_r)
-ORDER = [15, -15, 12, -12, 6, -6, 9, -9, 3, -3, 0]
-FIRST = [r for q in ORDER for r in CHILDREN[q] if r % 3]
-SECOND = [15, -15, 12, -12, 6, -6, 3, -3]
-THIRD = [9, -9]
-HOPS = FIRST + SECOND + THIRD
+LEAVES = [-16, -15, -13, 13, 15, -7, 7, -8, 8, -6, 6, -12, 12, -11, 11, -3, 3]
+INNER = [14, -14, 5, -5, 2, -2, -9, 9, 4, -4, 1, -1, -10, 10]
+HOPS = LEAVES + INNER
 HOP_AT = {r: i for i, r in enumerate(HOPS)}
-Z_NEAR = (1, -1, 3, -3, 6, -6)
+RELAY = 4
+Z_NEAR = (1, -1, 2, -2, 3, -3, RELAY, -RELAY)
 
 
 def kernel(
@@ -53,7 +50,7 @@
     sx, rx, sg, rg, se, re, si, ri,
     hid, hid_t, act, rate,
     own, sc, rc, hop_s, hop_r,
-    load_sem, x_sem, g_sem, e_sem, i_sem, c_sem, h_sem,
+    load_sem, x_sem, g_sem, e_sem, i_sem, c_sem, h_sem, relay_sem,
 ):
     dp, ex = lax.axis_index("dp"), lax.axis_index("expert")
     z_count = lax.axis_size("dp") // 2
@@ -66,12 +63,6 @@
 
     def at_z(shift):
         return (lax.rem(z + shift + z_count, z_count) * 2 + c, ex)
-
-    barrier = pltpu.get_barrier_semaphore()
-    greeted = [(dp, at_place(j, 1)) for j in range(1, SLOTS)]
-    greeted += [at_z(d) for d in Z_NEAR] + [(z * 2 + 1 - c, ex)]
-    for device in greeted:
-        pl.semaphore_signal(barrier, inc=1, device_id=device, device_id_type=MESH)
 
     loads = [
         pltpu.make_async_copy(source, target, load_sem.at[i])
@@ -80,8 +71,15 @@
              (wg_hbm, wg), (wu_hbm, wu), (wd_hbm, wd))
         )
     ]
-    for load in loads:
+    for load in loads[:4]:
         load.start()
+
+    barrier = pltpu.get_barrier_semaphore()
+    greeted = [(dp, at_place(j, 1)) for j in range(1, SLOTS)]
+    greeted += [at_z(d) for d in Z_NEAR] + [(z * 2 + 1 - c, ex)]
+    for device in greeted:
+        pl.semaphore_signal(barrier, inc=1, device_id=device, device_id_type=MESH)
+
     loads[0].wait()
     loads[1].wait()
 
@@ -111,10 +109,7 @@
 
     whole = SLOTS * CAP
     width = lat.shape[1]
-    loads[2].wait()
-    picked = place[...].reshape(whole, tokens)
-    sx[...] = jnp.dot(picked, lat[...], preferred_element_type=F32).astype(BF16).reshape(
-        SLOTS, CAP, width)
+    parts = [slice(g * GROUP, (g + 1) * GROUP) for g in reversed(range(GROUPS))]
 
     def send(source, target, sems, j, sign):
         copy = pltpu.make_async_remote_copy(
@@ -123,14 +118,32 @@
         copy.start()
         return copy
 
-    pl.semaphore_wait(barrier, len(greeted))
-    x_copies = {j: send(sx, rx, x_sem, j, 1) for j in FAR_FIRST}
+    def send_part(copies, source, target, sems, part, sign):
+        for j in reversed(range(part.start, part.stop)):
+            if j:
+                copies[j] = send(source, target, sems, j, sign)
+
+    x_copies, g_copies, e_copies, i_copies = {}, {}, {}, {}
+    loads[2].wait()
+    loads[3].wait()
+    for load in loads[4:]:
+        load.start()
+    for n, part in enumerate(parts):
+        picked = place[part].reshape(ROWS, tokens)
+        sx[part] = jnp.dot(picked, lat[...], preferred_element_type=F32).astype(BF16).reshape(
+            GROUP, CAP, width)
+        if n == 0:
+            pl.semaphore_wait(barrier, len(greeted))
+        send_part(x_copies, sx, rx, x_sem, part, 1)
+    for part in parts:
+        picked = place[part].reshape(ROWS, tokens)
+        row_weight = jnp.sum(place_w[part].reshape(ROWS, tokens), axis=1, keepdims=True)
+        scaled = row_weight * jnp.dot(picked, cot[...], preferred_element_type=F32)
+        sg[part] = scaled.astype(BF16).reshape(GROUP, CAP, width)
+        send_part(g_copies, sg, rg, g_sem, part, 1)
+    for shift in (RELAY, -RELAY):
+        pl.semaphore_signal(relay_sem, inc=1, device_id=at_z(shift), device_id_type=MESH)
     rx[0] = sx[0]
-    loads[3].wait()
-    row_weight = jnp.sum(place_w[...].reshape(whole, tokens), axis=1, keepdims=True)
-    scaled = row_weight * jnp.dot(picked, cot[...], preferred_element_type=F32)
-    sg[...] = scaled.astype(BF16).reshape(SLOTS, CAP, width)
-    g_copies = {j: send(sg, rg, g_sem, j, 1) for j in FAR_FIRST}
     rg[0] = sg[0]
 
     spread_w = place_w[...].reshape(whole, tokens).T
@@ -142,8 +155,7 @@
         load.wait()
     hidden_width = wg.shape[1]
     tile = 256
-    e_copies, i_copies = {}, {}
-    for g in range(GROUPS):
+    for g in reversed(range(GROUPS)):
         members = range(g * GROUP, (g + 1) * GROUP)
         for j in members:
             if j:
@@ -166,9 +178,6 @@
             hid_t[1, chunk, :, span] = turned[:, 1]
         result = jnp.dot(hid[...], wd[...], preferred_element_type=F32)
         se[g * GROUP:(g + 1) * GROUP] = result.astype(BF16).reshape(GROUP, CAP, width)
-        for j in reversed(members):
-            if j:
-                e_copies[j] = send(se, re, e_sem, j, -1)
     re[0] = se[0]
 
     for j in range(1, SLOTS):
@@ -186,13 +195,14 @@
             device_id=(z * 2 + 1 - c, ex), device_id_type=MESH)
         copy.start()
         c_copies.append(copy)
+    for part in parts:
+        send_part(e_copies, se, re, e_sem, part, -1)
     for i in range(2):
         part = slice(i * half, (i + 1) * half)
         lhs = hid_t[c, part].reshape(half * 16, whole)
         own[part] = jnp.dot(lhs, grads, preferred_element_type=F32).reshape(half, 16, width)
 
     def backward(g):
-        members = range(g * GROUP, (g + 1) * GROUP)
         span = slice(g * ROWS, (g + 1) * ROWS)
         row_grad = rg[g * GROUP:(g + 1) * GROUP].reshape(ROWS, width)
         total = jnp.zeros((ROWS, width), F32)
@@ -205,9 +215,7 @@
             total += lax.dot_general(gate_grad, wg[:, cols], turn, preferred_element_type=F32)
             total += lax.dot_general(up_grad, wu[:, cols], turn, preferred_element_type=F32)
         si[g * GROUP:(g + 1) * GROUP] = total.astype(BF16).reshape(GROUP, CAP, width)
-        for j in reversed(members):
-            if j:
-                i_copies[j] = send(si, ri, i_sem, j, -1)
+        send_part(i_copies, si, ri, i_sem, slice(g * GROUP, (g + 1) * GROUP), -1)
 
     hops = {}
 
@@ -228,14 +236,15 @@
         copy.start()
         hops[r] = copy
 
-    backward(0)
+    backward(1)
+    pl.semaphore_wait(relay_sem, 2)
     for copy in c_copies:
         copy.wait_recv()
-    for r in FIRST:
+    for r in LEAVES:
         hop(r)
-    backward(1)
+    backward(0)
     ri[0] = si[0]
-    for r in SECOND:
+    for r in INNER:
         hop(r)
     for j in range(1, SLOTS):
         e_copies[j].wait_recv()
@@ -243,8 +252,6 @@
     summed = jnp.dot(high, returned, preferred_element_type=F32)
     summed += jnp.dot(low, returned, preferred_element_type=F32)
     out_ref[...] = summed.astype(BF16)
-    for r in THIRD:
-        hop(r)
     for j in range(1, SLOTS):
         i_copies[j].wait_recv()
     grad_ref[...] = jnp.dot(
@@ -271,9 +278,9 @@
     latent_out, grad_latents, grad_down = pl.pallas_call(
         kernel,
         out_shape=(
-            jax.ShapeDtypeStruct((tokens, width), BF16),
-            jax.ShapeDtypeStruct((tokens, width), BF16),
-            jax.ShapeDtypeStruct((16, width), F32),
+            pltpu.VMEM((tokens, width), BF16),
+            pltpu.VMEM((tokens, width), BF16),
+            pltpu.VMEM((16, width), F32),
         ),
         in_specs=[anywhere] * 7,
         out_specs=(in_vmem,) * 3,
@@ -300,7 +307,7 @@
             pltpu.VMEM((hop_count, 16, width), BF16),
             pltpu.VMEM((hop_count, 16, width), BF16),
             dma((7,)), dma((2, SLOTS)), dma((2, SLOTS)), dma((2, SLOTS)), dma((2, SLOTS)),
-            dma((2, 2)), dma((2, hop_count)),
+            dma((2, 2)), dma((2, hop_count)), pltpu.SemaphoreType.REGULAR,
         ],
         compiler_params=pltpu.CompilerParams(
             collective_id=0, has_side_effects=True, vmem_limit_bytes=56 << 20),

time: 67.9 us -> 63.5 us (0.935)
  the two profiles are of different devices: /device:TPU:14 before, /device:TPU:32 now
where the time goes in v2:
time: 63.5 us; the launch traced here: 63.4 us
  Pallas kernels  60.8 us (96%)
  local copies, waits for them, and re-layouts  1.93 us (3%)
  between operations  0.64 us (1%)
    pallas_call x1, Pallas kernels, local(): pl.pallas_call(kernel, out_shape=(pltpu.VMEM((tokens, width), BF16), pltp...  60.8 us
    unnamed x3, local copies, waits for them, and re-layouts  1.93 us

profile of v2, /device:TPU:32, one launch (start us, length us, event | category | flops | bytes accessed | tf_op | source)
XLA Modules:
  0.0 63.4 jit_solution(544208079291932796)
XLA Ops:
  0.6 60.8 %moe.1 = (bf16[128,512]{1,0:T(8,128)(2,1)S(1)}, bf16[128,512]{1,0:T(8,128)(2,1)S(1)}, f32[16,512]{1,0:T(8,128)S(1)}) custom-call(bf16[128,512]{1,0:T(8,128)(2,1)} %lat_hbm.1, s32[3,128]{1,0:T(4,128)} %bitcast.10, s32[3,128]{1,0:T(4,128)} %bitcast.11, bf16[128,512]{1,0:T(8,128)(2,1)} %cot_hbm.1, bf16[512,1024]{1,0:T(8,128)(2,1)} %bitcast.7, ...), custom_call_target="tpu_custom_call" | custom-call | tf_op jit(solution)/shard_map/moe/pallas_call | solution.py:278
  61.4 0.7 %copy.13 = bf16[128,512]{1,0:T(8,128)(2,1)} copy(bf16[128,512]{1,0:T(8,128)(2,1)S(1)} %get-tuple-element.9) | data formatting | bytes 262144
  62.1 0.6 copy.15
  62.7 0.7 %copy.14 = bf16[128,512]{1,0:T(8,128)(2,1)} copy(bf16[128,512]{1,0:T(8,128)(2,1)S(1)} %get-tuple-element.10) | data formatting | bytes 262144

commit v3 on v2

--- a/solution.py
+++ b/solution.py
@@ -38,6 +38,8 @@
 INNER = [14, -14, 5, -5, 2, -2, -9, 9, 4, -4, 1, -1, -10, 10]
 HOPS = LEAVES + INNER
 HOP_AT = {r: i for i, r in enumerate(HOPS)}
+PIECES = 2
+LATER = [(0, -14), (0, 14), (0, -9), (0, 9), (0, -5), (0, 5), (0, -2), (0, 2), (1, 14), (1, -14), (1, -9), (1, 5), (1, -5), (1, 9), (1, 2), (1, -2), (0, 4), (0, -4), (0, 1), (0, -1), (0, 10), (0, -10), (1, 4), (1, -4), (1, 10), (1, -10), (1, 1), (1, -1)]
 RELAY = 4
 Z_NEAR = (1, -1, 2, -2, 3, -3, RELAY, -RELAY)
 
@@ -123,7 +125,9 @@
             if j:
                 copies[j] = send(source, target, sems, j, sign)
 
-    x_copies, g_copies, e_copies, i_copies = {}, {}, {}, {}
+    x_copies, e_copies, i_copies = {}, {}, {}
+    g_copies = [{} for _ in range(PIECES)]
+    piece = width // PIECES
     loads[2].wait()
     loads[3].wait()
     for load in loads[4:]:
@@ -139,12 +143,18 @@
         picked = place[part].reshape(ROWS, tokens)
         row_weight = jnp.sum(place_w[part].reshape(ROWS, tokens), axis=1, keepdims=True)
         scaled = row_weight * jnp.dot(picked, cot[...], preferred_element_type=F32)
-        sg[part] = scaled.astype(BF16).reshape(GROUP, CAP, width)
-        send_part(g_copies, sg, rg, g_sem, part, 1)
+        scaled = scaled.astype(BF16)
+        for p in range(PIECES):
+            sg[p, part] = scaled[:, p * piece:(p + 1) * piece].reshape(GROUP, CAP, piece)
+        send_part(g_copies[0], sg.at[0], rg.at[0], g_sem.at[0], part, 1)
+    for p in range(1, PIECES):
+        for part in parts:
+            send_part(g_copies[p], sg.at[p], rg.at[p], g_sem.at[p], part, 1)
     for shift in (RELAY, -RELAY):
         pl.semaphore_signal(relay_sem, inc=1, device_id=at_z(shift), device_id_type=MESH)
     rx[0] = sx[0]
-    rg[0] = sg[0]
+    for p in range(PIECES):
+        rg[p, 0] = sg[p, 0]
 
     spread_w = place_w[...].reshape(whole, tokens).T
     high = spread_w.astype(BF16)
@@ -180,36 +190,34 @@
         se[g * GROUP:(g + 1) * GROUP] = result.astype(BF16).reshape(GROUP, CAP, width)
     re[0] = se[0]
 
-    for j in range(1, SLOTS):
-        g_copies[j].wait_recv()
-    grads = rg[...].reshape(whole, width)
-    half = z_count // 2
-    c_copies = []
-    for i in range(2):
-        part = slice(i * half, (i + 1) * half)
-        lhs = hid_t[1 - c, part].reshape(half * 16, whole)
+    c_copies = {}
+
+    def down(p):
+        for j in range(1, SLOTS):
+            g_copies[p][j].wait_recv()
+        grads = rg[p].reshape(whole, piece)
+        lhs = hid_t[1 - c].reshape(z_count * 16, whole)
         term = jnp.dot(lhs, grads, preferred_element_type=F32)
-        sc[part] = term.astype(BF16).reshape(half, 16, width)
+        sc[p] = term.astype(BF16).reshape(z_count, 16, piece)
         copy = pltpu.make_async_remote_copy(
-            sc.at[part], rc.at[part], c_sem.at[0, i], c_sem.at[1, i],
+            sc.at[p], rc.at[p], c_sem.at[0, p], c_sem.at[1, p],
             device_id=(z * 2 + 1 - c, ex), device_id_type=MESH)
         copy.start()
-        c_copies.append(copy)
-    for part in parts:
-        send_part(e_copies, se, re, e_sem, part, -1)
-    for i in range(2):
-        part = slice(i * half, (i + 1) * half)
-        lhs = hid_t[c, part].reshape(half * 16, whole)
-        own[part] = jnp.dot(lhs, grads, preferred_element_type=F32).reshape(half, 16, width)
+        c_copies[p] = copy
+        lhs = hid_t[c].reshape(z_count * 16, whole)
+        own[p] = jnp.dot(lhs, grads, preferred_element_type=F32).reshape(z_count, 16, piece)
 
     def backward(g):
         span = slice(g * ROWS, (g + 1) * ROWS)
-        row_grad = rg[g * GROUP:(g + 1) * GROUP].reshape(ROWS, width)
+        row_grad = [rg[p, g * GROUP:(g + 1) * GROUP].reshape(ROWS, piece) for p in range(PIECES)]
         total = jnp.zeros((ROWS, width), F32)
         turn = (((1,), (1,)), ((), ()))
         for n in range(hidden_width // tile):
             cols = slice(n * tile, (n + 1) * tile)
-            back = lax.dot_general(row_grad, wd[cols, :], turn, preferred_element_type=F32)
+            back = jnp.zeros((ROWS, tile), F32)
+            for p in range(PIECES):
+                back += lax.dot_general(
+                    row_grad[p], wd[cols, p * piece:(p + 1) * piece], turn, preferred_element_type=F32)
             gate_grad = (back * rate[span, cols]).astype(BF16)
             up_grad = (back * act[span, cols]).astype(BF16)
             total += lax.dot_general(gate_grad, wg[:, cols], turn, preferred_element_type=F32)
@@ -219,33 +227,39 @@
 
     hops = {}
 
-    def partial(r):
+    def partial(p, r):
         d = lax.rem(z - r + z_count, z_count)
-        value = own[d] + rc[d].astype(F32)
+        value = own[p, d] + rc[p, d].astype(F32)
         for child in CHILDREN.get(r, ()):
-            hops[child].wait_recv()
-            value = value + hop_r[HOP_AT[child]].astype(F32)
+            hops[p, child].wait_recv()
+            value = value + hop_r[p, HOP_AT[child]].astype(F32)
         return value
 
-    def hop(r):
+    def hop(p, r):
         i = HOP_AT[r]
-        hop_s[i] = partial(r).astype(BF16)
+        hop_s[p, i] = partial(p, r).astype(BF16)
         copy = pltpu.make_async_remote_copy(
-            hop_s.at[i], hop_r.at[i], h_sem.at[0, i], h_sem.at[1, i],
+            hop_s.at[p, i], hop_r.at[p, i], h_sem.at[0, p, i], h_sem.at[1, p, i],
             device_id=at_z(PARENT[r] - r), device_id_type=MESH)
         copy.start()
-        hops[r] = copy
-
+        hops[p, r] = copy
+
+    down(0)
+    pl.semaphore_wait(relay_sem, 2)
+    c_copies[0].wait_recv()
+    for r in LEAVES:
+        hop(0, r)
+    down(1)
+    for part in parts:
+        send_part(e_copies, se, re, e_sem, part, -1)
     backward(1)
-    pl.semaphore_wait(relay_sem, 2)
-    for copy in c_copies:
-        copy.wait_recv()
+    c_copies[1].wait_recv()
     for r in LEAVES:
-        hop(r)
+        hop(1, r)
     backward(0)
     ri[0] = si[0]
-    for r in INNER:
-        hop(r)
+    for p, r in LATER:
+        hop(p, r)
     for j in range(1, SLOTS):
         e_copies[j].wait_recv()
     returned = re[...].reshape(whole, width)
@@ -256,13 +270,20 @@
         i_copies[j].wait_recv()
     grad_ref[...] = jnp.dot(
         spread_one, ri[...].reshape(whole, width), preferred_element_type=F32).astype(BF16)
-    down_ref[...] = partial(0)
-
-    for copies in (x_copies, g_copies, e_copies, i_copies, hops):
+    for p in range(PIECES):
+        down_ref[:, p * piece:(p + 1) * piece] = partial(p, 0)
+
+    for copies in (x_copies, *g_copies, e_copies, i_copies, c_copies, hops):
         for copy in copies.values():
             copy.wait_send()
-    for copy in c_copies:
-        copy.wait_send()
+
+
+def store(*refs):
+    copies = [pltpu.make_async_copy(refs[i], refs[3 + i], refs[6].at[i]) for i in range(3)]
+    for copy in copies:
+        copy.start()
+    for copy in copies:
+        copy.wait()
 
 
 def local(latents, routes, gate_level, cotangent, w_gate, w_up, w_down):
@@ -271,11 +292,13 @@
     whole = SLOTS * CAP
     z_count = lax.axis_size("dp") // 2
     block = (SLOTS, CAP, width)
+    piece = width // PIECES
+    sums = (PIECES, z_count, 16, piece)
     hop_count = len(HOPS)
     anywhere = pl.BlockSpec(memory_space=pl.ANY)
     in_vmem = pl.BlockSpec(memory_space=pltpu.VMEM)
     dma = pltpu.SemaphoreType.DMA
-    latent_out, grad_latents, grad_down = pl.pallas_call(
+    results = pl.pallas_call(
         kernel,
         out_shape=(
             pltpu.VMEM((tokens, width), BF16),
@@ -296,23 +319,32 @@
             pltpu.VMEM((SLOTS, tokens), F32),
             pltpu.VMEM((SLOTS, CAP, tokens), BF16),
             pltpu.VMEM((SLOTS, CAP, tokens), F32),
-        ] + [pltpu.VMEM(block, BF16)] * 8 + [
+        ] + [pltpu.VMEM(block, BF16)] * 2 + [pltpu.VMEM((PIECES, SLOTS, CAP, piece), BF16)] * 2 + [
+            pltpu.VMEM(block, BF16)] * 4 + [
             pltpu.VMEM((ROWS, hidden), BF16),
             pltpu.VMEM((2, z_count, 16, whole), BF16),
             pltpu.VMEM((whole, hidden), F32),
             pltpu.VMEM((whole, hidden), F32),
-            pltpu.VMEM((z_count, 16, width), F32),
-            pltpu.VMEM((z_count, 16, width), BF16),
-            pltpu.VMEM((z_count, 16, width), BF16),
-            pltpu.VMEM((hop_count, 16, width), BF16),
-            pltpu.VMEM((hop_count, 16, width), BF16),
-            dma((7,)), dma((2, SLOTS)), dma((2, SLOTS)), dma((2, SLOTS)), dma((2, SLOTS)),
-            dma((2, 2)), dma((2, hop_count)), pltpu.SemaphoreType.REGULAR,
+            pltpu.VMEM(sums, F32),
+            pltpu.VMEM(sums, BF16),
+            pltpu.VMEM(sums, BF16),
+            pltpu.VMEM((PIECES, hop_count, 16, piece), BF16),
+            pltpu.VMEM((PIECES, hop_count, 16, piece), BF16),
+            dma((7,)), dma((2, SLOTS)), dma((PIECES, 2, SLOTS)), dma((2, SLOTS)), dma((2, SLOTS)),
+            dma((2, PIECES)), dma((2, PIECES, hop_count)), pltpu.SemaphoreType.REGULAR,
         ],
         compiler_params=pltpu.CompilerParams(
             collective_id=0, has_side_effects=True, vmem_limit_bytes=56 << 20),
         name="moe",
     )(latents, routes.T, gate_level.T, cotangent, w_gate[0], w_up[0], w_down[0])
+    latent_out, grad_latents, grad_down = pl.pallas_call(
+        store,
+        out_shape=[jax.ShapeDtypeStruct(r.shape, r.dtype) for r in results],
+        in_specs=[anywhere] * 3,
+        out_specs=[anywhere] * 3,
+        scratch_shapes=[dma((3,))],
+        name="store",
+    )(*[pltpu.with_memory_space_constraint(r, pltpu.VMEM) for r in results])
     return latent_out, grad_latents, grad_down[None]
 
 

time: 63.5 us -> 60.1 us (0.946)
  local copies, waits for them, and re-layouts: 1.93 us -> 0 us
  Pallas kernels: 60.8 us -> 59.3 us
    pallas_call x1, Pallas kernels: 60.8 us -> 58.5 us  [local(): pl.pallas_call(kernel, out_shape=(pltpu.VMEM((tokens, width), BF16), pltp...]
    unnamed x3 -> x0, local copies, waits for them, and re-layouts: 1.93 us -> none
    pallas_call x0 -> x1, Pallas kernels: none -> 0.73 us  [local(): pl.pallas_call(store, out_shape=[jax.ShapeDtypeStruct(r.shape, r.dtype) f...]
where the time goes in v3:
time: 60.1 us; the launch traced here: 59.9 us
  Pallas kernels  59.3 us (99%)
  between operations  0.64 us (1%)
    pallas_call x1, Pallas kernels, local(): pl.pallas_call(kernel, out_shape=(pltpu.VMEM((tokens, width), BF16), pltp...  58.5 us

profile of v3, /device:TPU:32, one launch (start us, length us, event | category | flops | bytes accessed | tf_op | source)
XLA Modules:
  0.0 59.9 jit_solution(17926399121864664894)
XLA Ops:
  0.6 58.5 %moe.1 = (bf16[128,512]{1,0:T(8,128)(2,1)S(1)}, bf16[128,512]{1,0:T(8,128)(2,1)S(1)}, f32[16,512]{1,0:T(8,128)S(1)}) custom-call(bf16[128,512]{1,0:T(8,128)(2,1)} %lat_hbm.1, s32[3,128]{1,0:T(4,128)} %bitcast.9, s32[3,128]{1,0:T(4,128)} %bitcast.10, bf16[128,512]{1,0:T(8,128)(2,1)} %cot_hbm.1, bf16[512,1024]{1,0:T(8,128)(2,1)} %bitcast.6, ...), custom_call_target="tpu_custom_call" | custom-call | tf_op jit(solution)/shard_map/moe/pallas_call | solution.py:301
  59.2 0.7 %store.1 = (bf16[128,512]{1,0:T(8,128)(2,1)}, bf16[128,512]{1,0:T(8,128)(2,1)}, f32[16,512]{1,0:T(8,128)}) custom-call(bf16[128,512]{1,0:T(8,128)(2,1)S(1)} %get-tuple-element.9.refs_0_, bf16[128,512]{1,0:T(8,128)(2,1)S(1)} %get-tuple-element.10.refs_1_, f32[16,512]{1,0:T(8,128)S(1)} %get-tuple-element.11.refs_2_), custom_call_target="tpu_custom_call" | custom-call | tf_op jit(solution)/shard_map/store/pallas_call | solution.py:340

commit v4 on v3

--- a/solution.py
+++ b/solution.py
@@ -35,13 +35,13 @@
 for _r, _q in PARENT.items():
     CHILDREN.setdefault(_q, []).append(_r)
 LEAVES = [-16, -15, -13, 13, 15, -7, 7, -8, 8, -6, 6, -12, 12, -11, 11, -3, 3]
-INNER = [14, -14, 5, -5, 2, -2, -9, 9, 4, -4, 1, -1, -10, 10]
-HOPS = LEAVES + INNER
+PIECES = 2
+INNER_NEAR = [14, -14, 5, -5, 2, -2, -9, 9]
+INNER_FAR = [4, -4, 1, -1, -10, 10]
+HOPS = LEAVES + INNER_NEAR + INNER_FAR
 HOP_AT = {r: i for i, r in enumerate(HOPS)}
-PIECES = 2
-LATER = [(0, -14), (0, 14), (0, -9), (0, 9), (0, -5), (0, 5), (0, -2), (0, 2), (1, 14), (1, -14), (1, -9), (1, 5), (1, -5), (1, 9), (1, 2), (1, -2), (0, 4), (0, -4), (0, 1), (0, -1), (0, 10), (0, -10), (1, 4), (1, -4), (1, 10), (1, -10), (1, 1), (1, -1)]
-RELAY = 4
-Z_NEAR = (1, -1, 2, -2, 3, -3, RELAY, -RELAY)
+Z_NEAR = (1, -1, 2, -2)
+RELAYS = (2, 4)
 
 
 def kernel(
@@ -139,6 +139,12 @@
         if n == 0:
             pl.semaphore_wait(barrier, len(greeted))
         send_part(x_copies, sx, rx, x_sem, part, 1)
+
+    def relay(i):
+        for shift in (RELAYS[i], -RELAYS[i]):
+            pl.semaphore_signal(relay_sem.at[i], inc=1, device_id=at_z(shift), device_id_type=MESH)
+
+    relay(0)
     for part in parts:
         picked = place[part].reshape(ROWS, tokens)
         row_weight = jnp.sum(place_w[part].reshape(ROWS, tokens), axis=1, keepdims=True)
@@ -150,8 +156,8 @@
     for p in range(1, PIECES):
         for part in parts:
             send_part(g_copies[p], sg.at[p], rg.at[p], g_sem.at[p], part, 1)
-    for shift in (RELAY, -RELAY):
-        pl.semaphore_signal(relay_sem, inc=1, device_id=at_z(shift), device_id_type=MESH)
+    pl.semaphore_wait(relay_sem.at[0], 2)
+    relay(1)
     rx[0] = sx[0]
     for p in range(PIECES):
         rg[p, 0] = sg[p, 0]
@@ -245,21 +251,32 @@
         hops[p, r] = copy
 
     down(0)
-    pl.semaphore_wait(relay_sem, 2)
+    pl.semaphore_wait(relay_sem.at[1], 2)
     c_copies[0].wait_recv()
     for r in LEAVES:
         hop(0, r)
     down(1)
     for part in parts:
         send_part(e_copies, se, re, e_sem, part, -1)
-    backward(1)
     c_copies[1].wait_recv()
     for r in LEAVES:
         hop(1, r)
+    for p in range(PIECES):
+        for r in INNER_NEAR:
+            hop(p, r)
+    backward(1)
+    for r in INNER_FAR:
+        hop(0, r)
     backward(0)
     ri[0] = si[0]
-    for p, r in LATER:
-        hop(p, r)
+    for r in INNER_FAR:
+        hop(1, r)
+    for copies in (x_copies, *g_copies, c_copies):
+        for copy in copies.values():
+            copy.wait_send()
+    for p in range(PIECES):
+        for r in LEAVES + INNER_NEAR:
+            hops[p, r].wait_send()
     for j in range(1, SLOTS):
         e_copies[j].wait_recv()
     returned = re[...].reshape(whole, width)
@@ -270,12 +287,14 @@
         i_copies[j].wait_recv()
     grad_ref[...] = jnp.dot(
         spread_one, ri[...].reshape(whole, width), preferred_element_type=F32).astype(BF16)
-    for p in range(PIECES):
-        down_ref[:, p * piece:(p + 1) * piece] = partial(p, 0)
-
-    for copies in (x_copies, *g_copies, e_copies, i_copies, c_copies, hops):
+    for copies in (e_copies, i_copies):
         for copy in copies.values():
             copy.wait_send()
+    for p in range(PIECES):
+        down_ref[:, p * piece:(p + 1) * piece] = partial(p, 0)
+    for p in range(PIECES):
+        for r in INNER_FAR:
+            hops[p, r].wait_send()
 
 
 def store(*refs):
@@ -331,7 +350,7 @@
             pltpu.VMEM((PIECES, hop_count, 16, piece), BF16),
             pltpu.VMEM((PIECES, hop_count, 16, piece), BF16),
             dma((7,)), dma((2, SLOTS)), dma((PIECES, 2, SLOTS)), dma((2, SLOTS)), dma((2, SLOTS)),
-            dma((2, PIECES)), dma((2, PIECES, hop_count)), pltpu.SemaphoreType.REGULAR,
+            dma((2, PIECES)), dma((2, PIECES, hop_count)), pltpu.SemaphoreType.REGULAR((2,)),
         ],
         compiler_params=pltpu.CompilerParams(
             collective_id=0, has_side_effects=True, vmem_limit_bytes=56 << 20),

time: 60.1 us -> 59.4 us (0.988)
  the two profiles are of different devices: /device:TPU:32 before, /device:TPU:8 now
where the time goes in v4:
time: 59.4 us; the launch traced here: 59.2 us
  Pallas kernels  58.6 us (99%)
  between operations  0.64 us (1%)
    pallas_call x1, Pallas kernels, local(): pl.pallas_call(kernel, out_shape=(pltpu.VMEM((tokens, width), BF16), pltp...  57.9 us

profile of v4, /device:TPU:8, one launch (start us, length us, event | category | flops | bytes accessed | tf_op | source)
XLA Modules:
  0.0 59.2 jit_solution(16394544162292379072)
XLA Ops:
  0.6 57.9 %moe.1 = (bf16[128,512]{1,0:T(8,128)(2,1)S(1)}, bf16[128,512]{1,0:T(8,128)(2,1)S(1)}, f32[16,512]{1,0:T(8,128)S(1)}) custom-call(bf16[128,512]{1,0:T(8,128)(2,1)} %lat_hbm.1, s32[3,128]{1,0:T(4,128)} %bitcast.9, s32[3,128]{1,0:T(4,128)} %bitcast.10, bf16[128,512]{1,0:T(8,128)(2,1)} %cot_hbm.1, bf16[512,1024]{1,0:T(8,128)(2,1)} %bitcast.6, ...), custom_call_target="tpu_custom_call" | custom-call | tf_op jit(solution)/shard_map/moe/pallas_call | solution.py:320
  58.5 0.7 %store.1 = (bf16[128,512]{1,0:T(8,128)(2,1)}, bf16[128,512]{1,0:T(8,128)(2,1)}, f32[16,512]{1,0:T(8,128)}) custom-call(bf16[128,512]{1,0:T(8,128)(2,1)S(1)} %get-tuple-element.9.refs_0_, bf16[128,512]{1,0:T(8,128)(2,1)S(1)} %get-tuple-element.10.refs_1_, f32[16,512]{1,0:T(8,128)S(1)} %get-tuple-element.11.refs_2_), custom_call_target="tpu_custom_call" | custom-call | tf_op jit(solution)/shard_map/store/pallas_call | solution.py:359

commit v5 on v4

--- a/solution.py
+++ b/solution.py
@@ -38,8 +38,9 @@
 PIECES = 2
 INNER_NEAR = [14, -14, 5, -5, 2, -2, -9, 9]
 INNER_FAR = [4, -4, 1, -1, -10, 10]
-HOPS = LEAVES + INNER_NEAR + INNER_FAR
+HOPS = [r for q in CHILDREN for r in CHILDREN[q]]
 HOP_AT = {r: i for i, r in enumerate(HOPS)}
+PARENT_AT = {q: i for i, q in enumerate(CHILDREN)}
 Z_NEAR = (1, -1, 2, -2)
 RELAYS = (2, 4)
 
@@ -52,7 +53,7 @@
     sx, rx, sg, rg, se, re, si, ri,
     hid, hid_t, act, rate,
     own, sc, rc, hop_s, hop_r,
-    load_sem, x_sem, g_sem, e_sem, i_sem, c_sem, h_sem, relay_sem,
+    load_sem, x_sem, g_sem, e_sem, i_sem, c_sem, hop_sem, hop_sent, relay_sem,
 ):
     dp, ex = lax.axis_index("dp"), lax.axis_index("expert")
     z_count = lax.axis_size("dp") // 2
@@ -113,20 +114,25 @@
     width = lat.shape[1]
     parts = [slice(g * GROUP, (g + 1) * GROUP) for g in reversed(range(GROUPS))]
 
-    def send(source, target, sems, j, sign):
-        copy = pltpu.make_async_remote_copy(
-            source.at[j], target.at[j], sems.at[0, j], sems.at[1, j],
-            device_id=(dp, at_place(j, sign)), device_id_type=MESH)
-        copy.start()
-        return copy
-
-    def send_part(copies, source, target, sems, part, sign):
-        for j in reversed(range(part.start, part.stop)):
-            if j:
-                copies[j] = send(source, target, sems, j, sign)
-
-    x_copies, e_copies, i_copies = {}, {}, {}
-    g_copies = [{} for _ in range(PIECES)]
+    def send(source, target, send_sem, recv_sem, part, sign):
+        for j in reversed(range(max(part.start, 1), part.stop)):
+            pltpu.make_async_remote_copy(
+                source.at[j], target.at[j], send_sem, recv_sem,
+                device_id=(dp, at_place(j, sign)), device_id_type=MESH).start()
+
+    def bulk(source, target, send_sem, recv_sem):
+        return pltpu.make_async_remote_copy(
+            source, target, send_sem, recv_sem,
+            device_id=(dp, at_place(1, 1)), device_id_type=MESH)
+
+    def sent(source, send_sem, recv_sem):
+        bulk(source.at[1:], source.at[1:], send_sem, recv_sem).wait_send()
+
+    def arrived(target, send_sem, recv_sem, part):
+        rows = target.at[max(part.start, 1):part.stop]
+        bulk(rows, rows, send_sem, recv_sem).wait_recv()
+
+    every = slice(0, SLOTS)
     piece = width // PIECES
     loads[2].wait()
     loads[3].wait()
@@ -138,7 +144,7 @@
             GROUP, CAP, width)
         if n == 0:
             pl.semaphore_wait(barrier, len(greeted))
-        send_part(x_copies, sx, rx, x_sem, part, 1)
+        send(sx, rx, x_sem.at[0], x_sem.at[1 + n], part, 1)
 
     def relay(i):
         for shift in (RELAYS[i], -RELAYS[i]):
@@ -152,10 +158,9 @@
         scaled = scaled.astype(BF16)
         for p in range(PIECES):
             sg[p, part] = scaled[:, p * piece:(p + 1) * piece].reshape(GROUP, CAP, piece)
-        send_part(g_copies[0], sg.at[0], rg.at[0], g_sem.at[0], part, 1)
+        send(sg.at[0], rg.at[0], g_sem.at[0, 0], g_sem.at[1, 0], part, 1)
     for p in range(1, PIECES):
-        for part in parts:
-            send_part(g_copies[p], sg.at[p], rg.at[p], g_sem.at[p], part, 1)
+        send(sg.at[p], rg.at[p], g_sem.at[0, p], g_sem.at[1, p], every, 1)
     pl.semaphore_wait(relay_sem.at[0], 2)
     relay(1)
     rx[0] = sx[0]
@@ -172,10 +177,8 @@
     hidden_width = wg.shape[1]
     tile = 256
     for g in reversed(range(GROUPS)):
-        members = range(g * GROUP, (g + 1) * GROUP)
-        for j in members:
-            if j:
-                x_copies[j].wait_recv()
+        n = GROUPS - 1 - g
+        arrived(rx, x_sem.at[0], x_sem.at[1 + n], parts[n])
         rows_in = rx[g * GROUP:(g + 1) * GROUP].reshape(ROWS, width)
         span = slice(g * ROWS, (g + 1) * ROWS)
         for n in range(hidden_width // tile):
@@ -199,8 +202,7 @@
     c_copies = {}
 
     def down(p):
-        for j in range(1, SLOTS):
-            g_copies[p][j].wait_recv()
+        arrived(rg.at[p], g_sem.at[0, p], g_sem.at[1, p], every)
         grads = rg[p].reshape(whole, piece)
         lhs = hid_t[1 - c].reshape(z_count * 16, whole)
         term = jnp.dot(lhs, grads, preferred_element_type=F32)
@@ -229,26 +231,26 @@
             total += lax.dot_general(gate_grad, wg[:, cols], turn, preferred_element_type=F32)
             total += lax.dot_general(up_grad, wu[:, cols], turn, preferred_element_type=F32)
         si[g * GROUP:(g + 1) * GROUP] = total.astype(BF16).reshape(GROUP, CAP, width)
-        send_part(i_copies, si, ri, i_sem, slice(g * GROUP, (g + 1) * GROUP), -1)
-
-    hops = {}
+        send(si, ri, i_sem.at[0], i_sem.at[1], slice(g * GROUP, (g + 1) * GROUP), -1)
 
     def partial(p, r):
         d = lax.rem(z - r + z_count, z_count)
         value = own[p, d] + rc[p, d].astype(F32)
-        for child in CHILDREN.get(r, ()):
-            hops[p, child].wait_recv()
-            value = value + hop_r[p, HOP_AT[child]].astype(F32)
+        if r in CHILDREN:
+            first = HOP_AT[CHILDREN[r][0]]
+            last = first + len(CHILDREN[r])
+            rows = hop_r.at[p, first:last]
+            bulk(rows, rows, hop_sent, hop_sem.at[p, PARENT_AT[r]]).wait_recv()
+            for i in range(first, last):
+                value = value + hop_r[p, i].astype(F32)
         return value
 
     def hop(p, r):
         i = HOP_AT[r]
         hop_s[p, i] = partial(p, r).astype(BF16)
-        copy = pltpu.make_async_remote_copy(
-            hop_s.at[p, i], hop_r.at[p, i], h_sem.at[0, p, i], h_sem.at[1, p, i],
-            device_id=at_z(PARENT[r] - r), device_id_type=MESH)
-        copy.start()
-        hops[p, r] = copy
+        pltpu.make_async_remote_copy(
+            hop_s.at[p, i], hop_r.at[p, i], hop_sent, hop_sem.at[p, PARENT_AT[PARENT[r]]],
+            device_id=at_z(PARENT[r] - r), device_id_type=MESH).start()
 
     down(0)
     pl.semaphore_wait(relay_sem.at[1], 2)
@@ -256,8 +258,7 @@
     for r in LEAVES:
         hop(0, r)
     down(1)
-    for part in parts:
-        send_part(e_copies, se, re, e_sem, part, -1)
+    send(se, re, e_sem.at[0], e_sem.at[1], every, -1)
     c_copies[1].wait_recv()
     for r in LEAVES:
         hop(1, r)
@@ -271,30 +272,23 @@
     ri[0] = si[0]
     for r in INNER_FAR:
         hop(1, r)
-    for copies in (x_copies, *g_copies, c_copies):
-        for copy in copies.values():
-            copy.wait_send()
+    sent(sx, x_sem.at[0], x_sem.at[1])
     for p in range(PIECES):
-        for r in LEAVES + INNER_NEAR:
-            hops[p, r].wait_send()
-    for j in range(1, SLOTS):
-        e_copies[j].wait_recv()
+        sent(sg.at[p], g_sem.at[0, p], g_sem.at[1, p])
+        c_copies[p].wait_send()
+    arrived(re, e_sem.at[0], e_sem.at[1], every)
     returned = re[...].reshape(whole, width)
     summed = jnp.dot(high, returned, preferred_element_type=F32)
     summed += jnp.dot(low, returned, preferred_element_type=F32)
     out_ref[...] = summed.astype(BF16)
-    for j in range(1, SLOTS):
-        i_copies[j].wait_recv()
+    arrived(ri, i_sem.at[0], i_sem.at[1], every)
     grad_ref[...] = jnp.dot(
         spread_one, ri[...].reshape(whole, width), preferred_element_type=F32).astype(BF16)
-    for copies in (e_copies, i_copies):
-        for copy in copies.values():
-            copy.wait_send()
+    sent(se, e_sem.at[0], e_sem.at[1])
+    sent(si, i_sem.at[0], i_sem.at[1])
     for p in range(PIECES):
         down_ref[:, p * piece:(p + 1) * piece] = partial(p, 0)
-    for p in range(PIECES):
-        for r in INNER_FAR:
-            hops[p, r].wait_send()
+    bulk(hop_s, hop_s, hop_sent, hop_sem.at[0, 0]).wait_send()
 
 
 def store(*refs):
@@ -349,8 +343,8 @@
             pltpu.VMEM(sums, BF16),
             pltpu.VMEM((PIECES, hop_count, 16, piece), BF16),
             pltpu.VMEM((PIECES, hop_count, 16, piece), BF16),
-            dma((7,)), dma((2, SLOTS)), dma((PIECES, 2, SLOTS)), dma((2, SLOTS)), dma((2, SLOTS)),
-            dma((2, PIECES)), dma((2, PIECES, hop_count)), pltpu.SemaphoreType.REGULAR((2,)),
+            dma((7,)), dma((1 + GROUPS,)), dma((2, PIECES)), dma((2,)), dma((2,)),
+            dma((2, PIECES)), dma((PIECES, len(CHILDREN))), dma, pltpu.SemaphoreType.REGULAR((2,)),
         ],
         compiler_params=pltpu.CompilerParams(
             collective_id=0, has_side_effects=True, vmem_limit_bytes=56 << 20),

time: 59.4 us -> 57.2 us (0.963)
  Pallas kernels: 58.6 us -> 56.4 us
    pallas_call x1, Pallas kernels: 57.9 us -> 55.7 us  [local(): pl.pallas_call(kernel, out_shape=(pltpu.VMEM((tokens, width), BF16), pltp...]
where the time goes in v5:
time: 57.2 us; the launch traced here: 57 us
  Pallas kernels  56.4 us (99%)
  between operations  0.64 us (1%)
    pallas_call x1, Pallas kernels, local(): pl.pallas_call(kernel, out_shape=(pltpu.VMEM((tokens, width), BF16), pltp...  55.7 us

profile of v5, /device:TPU:8, one launch (start us, length us, event | category | flops | bytes accessed | tf_op | source)
XLA Modules:
  0.0 57.0 jit_solution(15163634527713857780)
XLA Ops:
  0.6 55.7 %moe.1 = (bf16[128,512]{1,0:T(8,128)(2,1)S(1)}, bf16[128,512]{1,0:T(8,128)(2,1)S(1)}, f32[16,512]{1,0:T(8,128)S(1)}) custom-call(bf16[128,512]{1,0:T(8,128)(2,1)} %lat_hbm.1, s32[3,128]{1,0:T(4,128)} %bitcast.9, s32[3,128]{1,0:T(4,128)} %bitcast.10, bf16[128,512]{1,0:T(8,128)(2,1)} %cot_hbm.1, bf16[512,1024]{1,0:T(8,128)(2,1)} %bitcast.6, ...), custom_call_target="tpu_custom_call" | custom-call | tf_op jit(solution)/shard_map/moe/pallas_call | solution.py:314
  56.3 0.7 %store.1 = (bf16[128,512]{1,0:T(8,128)(2,1)}, bf16[128,512]{1,0:T(8,128)(2,1)}, f32[16,512]{1,0:T(8,128)}) custom-call(bf16[128,512]{1,0:T(8,128)(2,1)S(1)} %get-tuple-element.9.refs_0_, bf16[128,512]{1,0:T(8,128)(2,1)S(1)} %get-tuple-element.10.refs_1_, f32[16,512]{1,0:T(8,128)S(1)} %get-tuple-element.11.refs_2_), custom_call_target="tpu_custom_call" | custom-call | tf_op jit(solution)/shard_map/store/pallas_call | solution.py:353

commit v6 on v5

--- a/solution.py
+++ b/solution.py
@@ -166,11 +166,6 @@
     rx[0] = sx[0]
     for p in range(PIECES):
         rg[p, 0] = sg[p, 0]
-
-    spread_w = place_w[...].reshape(whole, tokens).T
-    high = spread_w.astype(BF16)
-    low = (spread_w - high.astype(F32)).astype(BF16)
-    spread_one = place[...].astype(F32).reshape(whole, tokens).T.astype(BF16)
 
     for load in loads[4:]:
         load.wait()
@@ -258,10 +253,11 @@
     for r in LEAVES:
         hop(0, r)
     down(1)
-    send(se, re, e_sem.at[0], e_sem.at[1], every, -1)
+    send(se, re, e_sem.at[0], e_sem.at[1], parts[0], -1)
     c_copies[1].wait_recv()
     for r in LEAVES:
         hop(1, r)
+    send(se, re, e_sem.at[0], e_sem.at[1], parts[1], -1)
     for p in range(PIECES):
         for r in INNER_NEAR:
             hop(p, r)
@@ -272,6 +268,10 @@
     ri[0] = si[0]
     for r in INNER_FAR:
         hop(1, r)
+    spread_w = place_w[...].reshape(whole, tokens).T
+    high = spread_w.astype(BF16)
+    low = (spread_w - high.astype(F32)).astype(BF16)
+    spread_one = place[...].astype(F32).reshape(whole, tokens).T.astype(BF16)
     sent(sx, x_sem.at[0], x_sem.at[1])
     for p in range(PIECES):
         sent(sg.at[p], g_sem.at[0, p], g_sem.at[1, p])

time: 57.2 us -> 57.2 us (level)
  no operation moved by 1% of the time
where the time goes in v6:
time: 57.2 us; the launch traced here: 57 us
  Pallas kernels  56.4 us (99%)
  between operations  0.64 us (1%)
    pallas_call x1, Pallas kernels, local(): pl.pallas_call(kernel, out_shape=(pltpu.VMEM((tokens, width), BF16), pltp...  55.7 us

profile of v6, /device:TPU:8, one launch (start us, length us, event | category | flops | bytes accessed | tf_op | source)
XLA Modules:
  0.0 57.0 jit_solution(12407232462052174083)
XLA Ops:
  0.6 55.7 %moe.1 = (bf16[128,512]{1,0:T(8,128)(2,1)S(1)}, bf16[128,512]{1,0:T(8,128)(2,1)S(1)}, f32[16,512]{1,0:T(8,128)S(1)}) custom-call(bf16[128,512]{1,0:T(8,128)(2,1)} %lat_hbm.1, s32[3,128]{1,0:T(4,128)} %bitcast.9, s32[3,128]{1,0:T(4,128)} %bitcast.10, bf16[128,512]{1,0:T(8,128)(2,1)} %cot_hbm.1, bf16[512,1024]{1,0:T(8,128)(2,1)} %bitcast.6, ...), custom_call_target="tpu_custom_call" | custom-call | tf_op jit(solution)/shard_map/moe/pallas_call | solution.py:314
  56.3 0.7 %store.1 = (bf16[128,512]{1,0:T(8,128)(2,1)}, bf16[128,512]{1,0:T(8,128)(2,1)}, f32[16,512]{1,0:T(8,128)}) custom-call(bf16[128,512]{1,0:T(8,128)(2,1)S(1)} %get-tuple-element.9.refs_0_, bf16[128,512]{1,0:T(8,128)(2,1)S(1)} %get-tuple-element.10.refs_1_, f32[16,512]{1,0:T(8,128)S(1)} %get-tuple-element.11.refs_2_), custom_call_target="tpu_custom_call" | custom-call | tf_op jit(solution)/shard_map/store/pallas_call | solution.py:353
